TPU v7x, 32 devices: a whole 2x2x4 slice. The times are simulated.
32 devices in a mesh: line: 2 (over x), section: 16 (over z, y, core).
Axes of the slice: x: 2, y: 2, z: 4, core: 2. Of those that a mesh axis runs over, the one named last changes fastest.
Arguments:
- conductivity: float32 [256, 1024], P(('line', 'section')), parts along dimension 0, may hold values from 0.1 to 10
- forward_start: float32 [32, 4, 128, 1024], P('line', None, 'section'), parts along dimension 0, may hold values from -3 to 3
- adjoint_start: float32 [32, 4, 128, 1024], P('line', None, 'section'), parts along dimension 0, may hold values from -3 to 3
- source_cells: int32 [8, 2], P('line'), parts along dimension 0, may hold values from 0 to 131071
- receiver_cells: int32 [64, 2], P('line'), parts along dimension 0, may hold values from 0 to 131071
- observed: float32 [8, 32], P('line'), parts along dimension 0, may hold values from -60 to 60
- wavenumbers: float32 [16], replicated, may hold values from 0.02 to 2
- quadrature_weights: float32 [16], replicated, may hold values from 0.02 to 0.5
- receiver_offsets: float32 [32], replicated, may hold values from 0 to 4
Outputs:
- gradient: float32 [256, 1024], P(('line', 'section')), parts along dimension 0
- predicted: float32 [8, 32], P('line'), parts along dimension 0
- forward_field: float32 [32, 4, 128, 1024], P('line', None, 'section'), parts along dimension 0
There are 2 independent parts, one for each index of `line`. A program takes and returns all parts, laid end to end along the dimension named above; an argument that names none is the same for every part. Nothing has to cross between parts.
All inputs are finite; a program needn't handle non-finite values.
Results may differ from a plain program's by a relative error of at most 0.00002.
Values sent between devices are 32-bit elements; how exact they have to be, the bound alone decides.
A program may use at most 192 MiB of HBM per device.

v0:
```python
import jax
import jax.numpy as jnp
from jax import lax
from jax.sharding import PartitionSpec as P

SWEEPS = 3


OMEGA = 0.8
CURRENT = 10.0


def extended(block, sides, width):
    for axis, dim in sides:
        count = lax.axis_size(axis)
        forward = [(i, i + 1) for i in range(count - 1)]
        backward = [(target, source) for source, target in forward]
        low = lax.ppermute(
            lax.slice_in_dim(block, block.shape[dim] - width, None, axis=dim), axis, forward
        )
        high = lax.ppermute(lax.slice_in_dim(block, 0, width, axis=dim), axis, backward)
        block = jnp.concatenate([low, block, high], axis=dim)
    return block


def shifted(value, axis, steps):
    count = lax.axis_size(axis)
    first, last = (max(0, -steps), min(count, count - steps))
    return lax.ppermute(value, axis, [(source, source + steps) for source in range(first, last)])


def smooth_once(field_win, sigma_win, source_win, wave_sq, valid_rows):
    centre = sigma_win[1:-1]
    face_up = 0.5 * (centre + sigma_win[:-2])
    face_down = 0.5 * (centre + sigma_win[2:])
    side_pad = jnp.pad(centre, ((0, 0), (1, 1)))
    face_left = 0.5 * (centre + side_pad[:, :-2])
    face_right = 0.5 * (centre + side_pad[:, 2:])
    diag_terms = (face_up + face_down + face_left + face_right)[None] + wave_sq[
        :, None, None
    ] * centre[None]
    diag_terms = diag_terms + (1.0 - valid_rows)[None, :, None]
    middle = field_win[:, :, 1:-1]
    cols_pad = jnp.pad(middle, ((0, 0), (0, 0), (0, 0), (1, 1)))
    beside = face_up * field_win[:, :, :-2] + face_down * field_win[:, :, 2:]
    beside = beside + face_left * cols_pad[..., :-2] + face_right * cols_pad[..., 2:]
    updated = (1.0 - OMEGA) * middle + OMEGA * (source_win + beside) / diag_terms[:, None]
    return updated * valid_rows[:, None]


def local(
    conductivity,
    forward_start,
    adjoint_start,
    source_cells,
    receiver_cells,
    observed,
    wavenumbers,
    quadrature_weights,
    receiver_offsets,
):
    row_count = conductivity.shape[0]
    col_count = conductivity.shape[1]
    src_count = forward_start.shape[1]
    start = lax.axis_index("section") * row_count
    span_wide = row_count + 2 * SWEEPS
    wide_first = start - SWEEPS
    wave_sq = wavenumbers * wavenumbers
    sigma_wide = extended(conductivity, (("section", 0),), SWEEPS + 1)

    def sweep_all(field, source_wide):
        sigma_win = sigma_wide[SWEEPS : SWEEPS + row_count + 2]
        source_win = source_wide[:, :, SWEEPS : SWEEPS + row_count]
        valid_rows = jnp.ones((row_count,), jnp.float32)
        for sweep_index in range(SWEEPS):
            window = extended(field, (("section", 2),), 1)
            field = smooth_once(window, sigma_win, source_win, wave_sq, valid_rows)
        return field

    src_index = jnp.arange(source_cells.shape[0], dtype=jnp.int32)
    src_local = source_cells // col_count - wide_first
    src_cols = source_cells % col_count
    src_inside = (src_local >= 0) & (src_local < span_wide)
    src_safe = jnp.clip(src_local, 0, span_wide - 1)
    src_plus = jnp.where(src_inside[:, 0], CURRENT, 0.0).astype(jnp.float32)
    src_minus = jnp.where(src_inside[:, 1], -CURRENT, 0.0).astype(jnp.float32)
    forward_source = jnp.zeros((source_cells.shape[0], span_wide, col_count), jnp.float32)
    forward_source = forward_source.at[src_index, src_safe[:, 0], src_cols[:, 0]].add(src_plus)
    forward_source = forward_source.at[src_index, src_safe[:, 1], src_cols[:, 1]].add(src_minus)
    forward_field = sweep_all(forward_start, forward_source[None])
    coef = quadrature_weights[:, None] * jnp.cos(wavenumbers[:, None] * receiver_offsets[None, :])
    rec_rows = receiver_cells // col_count
    rec_cols = receiver_cells % col_count
    own_local = rec_rows - start
    own_inside = (own_local >= 0) & (own_local < row_count)
    own_safe = jnp.clip(own_local, 0, row_count - 1)
    at_m = jnp.where(
        own_inside[None, None, :, 0], forward_field[:, :, own_safe[:, 0], rec_cols[:, 0]], 0.0
    )
    at_n = jnp.where(
        own_inside[None, None, :, 1], forward_field[:, :, own_safe[:, 1], rec_cols[:, 1]], 0.0
    )
    partial_read = jnp.sum(coef[:, None, :] * (at_m - at_n), axis=0)
    predicted = lax.psum(partial_read, "section")
    amplitude = coef[:, None, :] * (predicted - observed)[None]
    wide_local = rec_rows - wide_first
    wide_inside = (wide_local >= 0) & (wide_local < span_wide)
    wide_safe = jnp.clip(wide_local, 0, span_wide - 1)
    plus_vals = jnp.where(wide_inside[None, None, :, 0], amplitude, 0.0)
    minus_vals = jnp.where(wide_inside[None, None, :, 1], -amplitude, 0.0)
    adjoint_source = jnp.zeros(forward_start.shape[:2] + (span_wide, col_count), jnp.float32)
    adjoint_source = adjoint_source.at[:, :, wide_safe[:, 0], rec_cols[:, 0]].add(plus_vals)
    adjoint_source = adjoint_source.at[:, :, wide_safe[:, 1], rec_cols[:, 1]].add(minus_vals)
    adjoint_field = sweep_all(adjoint_start, adjoint_source)
    fwd_next, adj_next = shifted((forward_field[:, :, :1], adjoint_field[:, :, :1]), "section", -1)
    zero_col = jnp.zeros(forward_field.shape[:3] + (1,), jnp.float32)
    fwd_row = jnp.concatenate([forward_field[:, :, 1:], fwd_next], axis=2) - forward_field
    adj_row = jnp.concatenate([adjoint_field[:, :, 1:], adj_next], axis=2) - adjoint_field
    fwd_col = jnp.concatenate([forward_field[..., 1:], zero_col], axis=3) - forward_field
    adj_col = jnp.concatenate([adjoint_field[..., 1:], zero_col], axis=3) - adjoint_field
    terms = (
        fwd_row * adj_row
        + fwd_col * adj_col
        + wave_sq[:, None, None, None] * forward_field * adjoint_field
    )
    gradient = jnp.sum(terms, axis=(0, 1)) / src_count
    return (gradient, predicted, forward_field)


def solution(mesh):
    placed = (
        P(("line", "section"), None),
        P("line", None, "section", None),
        P("line", None, "section", None),
        P("line", None),
        P("line", None),
        P("line", None),
        P(),
        P(),
        P(),
    )
    return jax.shard_map(
        local,
        mesh=mesh,
        in_specs=placed,
        out_specs=(P(("line", "section"), None), P("line", None), P("line", None, "section", None)),
        check_vma=False,
    )
```

profile of v0, /device:TPU:1, one launch (start us, length us, event | category | flops | bytes accessed | tf_op | source)
XLA Modules:
  0.0 240.3 jit_solution(6530539113647594805)
XLA Ops:
  0.6 0.8 fusion.115
  1.5 4.5 %collective-permute-start = (f32[4,1024]{1,0:T(4,128)S(1)}, f32[4,1024]{1,0:T(4,128)S(1)}, u32[]{:S(2)}, u32[]{:S(2)}) collective-permute-start(f32[4,1024]{1,0:T(4,128)S(1)} %get-tuple-element.44), channel_id=1, source_target_pairs={{0,1},{1,2},{2,3},{3,4},{4,5},{5,6},{6,7},{7,8},{8,9},{9,10},{10,1... | collective-permute-start | bytes 49160 | tf_op jit(solution)/shard_map/ppermute | solution.py:18
  6.0 1.9 collective-permute-start.2
  7.9 2.8 %fusion.114 = (f32[16,4,1,1024]{3,2,1,0:T(1,128)S(1)}, f32[16,4,1,1024]{3,2,1,0:T(1,128)S(1)}) fusion(f32[16,4,8,1024]{3,2,1,0:T(8,128)} %param.10), kind=kLoop, calls=%fused_computation.203 | loop fusion | bytes 1048576 | tf_op jit(solution)/shard_map/slice | solution.py:19
  10.9 3.6 %collective-permute-start.1 = (f32[16,4,1,1024]{3,0,2,1:T(8,128)S(1)}, f32[16,4,1,1024]{3,0,2,1:T(8,128)}, u32[]{:S(2)}, u32[]{:S(2)}) collective-permute-start(f32[16,4,1,1024]{3,0,2,1:T(8,128)S(1)} %copy.269), channel_id=1, source_target_pairs={{0,1},{1,2},{2,3},{3,4},{4,5},{5,6},{6,7},{7,8},{8,9},{9,10},{10,1... | collective-permute-start | bytes 786440 | tf_op jit(solution)/shard_map/ppermute | solution.py:18
  14.5 0.9 copy.270
  15.4 2.0 collective-permute-start.3
  17.4 2.7 %fusion.111 = (f32[16,4,1,1024]{3,2,1,0:T(1,128)S(1)}, f32[16,4,1,1024]{3,2,1,0:T(1,128)S(1)}) fusion(f32[16,4,8,1024]{3,2,1,0:T(8,128)} %param.11), kind=kLoop, calls=%fused_computation.200 | loop fusion | bytes 1048576 | tf_op jit(solution)/shard_map/slice | solution.py:19
  20.2 0.9 copy.272
  21.1 3.6 %collective-permute-start.9 = (f32[16,4,1,1024]{3,0,2,1:T(8,128)}, f32[16,4,1,1024]{3,0,2,1:T(8,128)}, u32[]{:S(2)}, u32[]{:S(2)}) collective-permute-start(f32[16,4,1,1024]{3,0,2,1:T(8,128)} %copy.272), channel_id=1, source_target_pairs={{0,1},{1,2},{2,3},{3,4},{4,5},{5,6},{6,7},{7,8},{8,9},{9,10},{10,1... | collective-permute-start | bytes 786440 | tf_op jit(solution)/shard_map/ppermute | solution.py:18
  24.9 0.7 scatter_fusion
  25.6 0.7 scatter_fusion.1
  26.5 0.9 copy.273
  27.4 1.9 collective-permute-start.10
  29.5 1.2 copy.237
  30.8 1.2 copy.239
  32.0 2.0 fusion.6
  34.6 3.6 %collective-permute-start.4 = (f32[16,4,1,1024]{3,0,2,1:T(8,128)S(1)}, f32[16,4,1,1024]{3,0,2,1:T(8,128)S(1)}, u32[]{:S(2)}, u32[]{:S(2)}) collective-permute-start(f32[16,4,1,1024]{3,0,2,1:T(8,128)S(1)} %copy.240), channel_id=1, source_target_pairs={{0,1},{1,2},{2,3},{3,4},{4,5},{5,6},{6,7},{7,8},{8,9},{9,10},{10,1... | collective-permute-start | bytes 786440 | tf_op jit(solution)/shard_map/ppermute | solution.py:18
  38.5 1.9 collective-permute-start.5
  40.4 1.2 collective-permute-done.4
  41.9 4.3 %collective-permute-done.5 = f32[16,4,1,1024]{3,0,2,1:T(8,128)S(1)} collective-permute-done((f32[16,4,1,1024]{3,0,2,1:T(8,128)S(1)}, f32[16,4,1,1024]{3,0,2,1:T(8,128)S(1)}, u32[]{:S(2)}, u32[]{:S(2)}) %collective-permute-start.5) | collective-permute-done | bytes 262176 | tf_op jit(solution)/shard_map/ppermute | solution.py:21
  46.4 2.0 fusion.14
  48.4 1.3 copy-done.4
  50.4 1.9 collective-permute-start.6
  52.5 2.4 %collective-permute-start.7 = (f32[16,4,1,1024]{3,0,2,1:T(8,128)S(1)}, f32[16,4,1,1024]{3,0,2,1:T(8,128)S(1)}, u32[]{:S(2)}, u32[]{:S(2)}) collective-permute-start(f32[16,4,1,1024]{3,0,2,1:T(8,128)S(1)} %copy.246), channel_id=1, source_target_pairs={{1,0},{2,1},{3,2},{4,3},{5,4},{6,5},{7,6},{8,7},{9,8},{10,9},{11,1... | collective-permute-start | bytes 786440 | tf_op jit(solution)/shard_map/ppermute | solution.py:21
  55.7 2.1 copy.255
  57.8 1.9 copy.257
  60.0 3.7 %collective-permute-done.7 = f32[16,4,1,1024]{3,0,2,1:T(8,128)S(1)} collective-permute-done((f32[16,4,1,1024]{3,0,2,1:T(8,128)S(1)}, f32[16,4,1,1024]{3,0,2,1:T(8,128)S(1)}, u32[]{:S(2)}, u32[]{:S(2)}) %collective-permute-start.7) | collective-permute-done | bytes 262176 | tf_op jit(solution)/shard_map/ppermute | solution.py:21
  64.0 2.0 fusion.22
  66.0 8.6 %copy.250 = f32[16,4,8,1024]{0,1,3,2:T(4,128)} copy(f32[16,4,8,1024]{3,2,1,0:T(8,128)S(1)} %fusion.22) | data formatting | bytes 4194304 | tf_op jit(solution)/shard_map/add | solution.py:47
  74.5 6.4 %gather_fusion = f32[32,16,4]{1,2,0:T(4,128)S(1)} fusion(f32[16,4,8,1024]{0,1,3,2:T(4,128)} %copy.250, s32[32]{0:T(128)S(1)} %get-tuple-element.53), kind=kCustom, calls=%fused_computation | custom fusion | bytes 16640 | tf_op jit(solution)/shard_map/gather | solution.py:98
  80.9 7.1 %gather_fusion.1 = f32[32,16,4]{1,2,0:T(4,128)} fusion(f32[16,4,8,1024]{0,1,3,2:T(4,128)} %copy.250, s32[32]{0:T(128)S(1)} %get-tuple-element.52), kind=kCustom, calls=%fused_computation.1 | custom fusion | bytes 16640 | tf_op jit(solution)/shard_map/gather | solution.py:101
  88.0 1.1 fusion.73
  89.0 54.2 %psum.7 = f32[4,32]{0,1:T(8,128)S(1)} all-reduce(f32[4,32]{0,1:T(8,128)S(1)} %fusion.73), channel_id=1, replica_groups=mesh['line'=2,'section'=16] {'section'}, use_global_device_ids=true, to_apply=%region_3.4 | all-reduce | flops 128 | bytes 1024 | tf_op jit(solution)/shard_map/psum | solution.py:104
  143.3 1.5 fusion.72
  144.7 9.8 %broadcast_in_dim.61 = f32[16,4,14,1024]{0,1,3,2:T(4,128)} broadcast(f32[]{:T(128)} %constant.36.clone.1), dimensions={} | broadcast | bytes 3670020 | tf_op jit(solution)/shard_map/broadcast_in_dim | solution.py:111
  154.5 3.9 %scatter_fusion.2 = f32[16,4,14,1024]{0,1,3,2:T(4,128)} fusion(f32[16,4,14,1024]{0,1,3,2:T(4,128)} %broadcast_in_dim.61, s32[32]{0:T(128)S(1)} %get-tuple-element.47, f32[32,16,4]{1,2,0:T(4,128)} %get-tuple-element.43), kind=kCustom, calls=%fused_computation.4 | custom fusion | flops 2048 | bytes 24832 | tf_op jit(solution)/shard_map/scatter-add | solution.py:112
  158.4 3.7 %scatter_fusion.3 = f32[16,4,14,1024]{0,1,3,2:T(4,128)} fusion(f32[16,4,14,1024]{0,1,3,2:T(4,128)} %scatter_fusion.2, s32[32]{0:T(128)S(1)} %get-tuple-element.46, f32[32,16,4]{1,2,0:T(4,128)S(1)} %get-tuple-element.42), kind=kCustom, calls=%fused_computation.5 | custom fusion | flops 2048 | bytes 24832 | tf_op jit(solution)/shard_map/scatter-add | solution.py:113
  162.1 13.7 %slice.332 = f32[16,4,8,1024]{0,1,3,2:T(4,128)} slice(f32[16,4,14,1024]{0,1,3,2:T(4,128)} %scatter_fusion.3), slice={[0:16], [0:4], [3:11], [0:1024]} | slice | bytes 4194304 | tf_op jit(solution)/shard_map/slice | solution.py:73
  175.8 11.0 %copy.271 = f32[16,4,8,1024]{3,2,1,0:T(8,128)} copy(f32[16,4,8,1024]{0,1,3,2:T(4,128)} %slice.332) | data formatting | bytes 4194304
  186.8 7.2 %fusion.30 = f32[16,4,8,1024]{3,2,1,0:T(8,128)S(1)} fusion(f32[16,4,8,1024]{3,2,1,0:T(8,128)} %copy.271, f32[16,4,8,1024]{3,2,1,0:T(8,128)} %param.11, f32[16,4,1,1024]{3,2,1,0:T(1,128)} %copy.257, f32[16,4,1,1024]{3,2,1,0:T(1,128)} %copy.255, f32[16,8,1024]{2,1,0:T(8,128)S(1)} %multiply_add_fusion, f32[8,1024]{1,0:T(8,128)S(1)} %get-tuple-element.29, ...), kind=kLoop, calls=%fused_computation.48 | loop fusion | flops 7340032 | bytes 7471104 | tf_op jit(solution)/shard_map/add | solution.py:47
  194.7 3.6 %collective-permute-start.11 = (f32[16,4,1,1024]{3,0,2,1:T(8,128)S(1)}, f32[16,4,1,1024]{3,0,2,1:T(8,128)S(1)}, u32[]{:S(2)}, u32[]{:S(2)}) collective-permute-start(f32[16,4,1,1024]{3,0,2,1:T(8,128)S(1)} %copy.258), channel_id=1, source_target_pairs={{0,1},{1,2},{2,3},{3,4},{4,5},{5,6},{6,7},{7,8},{8,9},{9,10},{10,1... | collective-permute-start | bytes 786440 | tf_op jit(solution)/shard_map/ppermute | solution.py:18
  198.5 4.6 %collective-permute-start.12 = (f32[16,4,1,1024]{3,0,2,1:T(8,128)S(1)}, f32[16,4,1,1024]{3,0,2,1:T(8,128)S(1)}, u32[]{:S(2)}, u32[]{:S(2)}) collective-permute-start(f32[16,4,1,1024]{3,0,2,1:T(8,128)S(1)} %copy.260), channel_id=1, source_target_pairs={{1,0},{2,1},{3,2},{4,3},{5,4},{6,5},{7,6},{8,7},{9,8},{10,9},{11,1... | collective-permute-start | bytes 786440 | tf_op jit(solution)/shard_map/ppermute | solution.py:21
  203.1 1.3 collective-permute-done.11
  204.7 1.5 collective-permute-done.12
  206.5 2.0 fusion.38
  209.1 2.9 %collective-permute-start.13 = (f32[16,4,1,1024]{3,0,2,1:T(8,128)S(1)}, f32[16,4,1,1024]{3,0,2,1:T(8,128)S(1)}, u32[]{:S(2)}, u32[]{:S(2)}) collective-permute-start(f32[16,4,1,1024]{3,0,2,1:T(8,128)S(1)} %copy.262), channel_id=1, source_target_pairs={{0,1},{1,2},{2,3},{3,4},{4,5},{5,6},{6,7},{7,8},{8,9},{9,10},{10,1... | collective-permute-start | bytes 786440 | tf_op jit(solution)/shard_map/ppermute | solution.py:18
  212.2 1.9 collective-permute-start.14
  214.3 0.9 copy.248
  215.2 1.9 collective-permute-start.8
  217.1 1.0 collective-permute-done.13
  218.5 1.5 collective-permute-done.14
  220.2 2.0 fusion.46
  222.4 1.1 copy.266
  223.5 2.1 collective-permute-start.15
  225.7 1.6 slice.330
  227.3 2.0 slice.339
  229.2 0.7 copy.268
  229.9 1.2 copy.249
  231.1 2.0 slice.337
  233.3 0.6 slice.340
  233.9 1.5 copy.267
  235.8 3.9 %fusion.69 = f32[8,1024]{1,0:T(8,128)S(1)} fusion(f32[16,4,1,1024]{3,2,1,0:T(1,128)S(1)} %copy.249, f32[16,4,7,1024]{3,2,1,0:T(8,128)S(1)} %copy-done.7, f32[16,4,8,1024]{3,2,1,0:T(8,128)S(1)} %copy-done.2, f32[16,4,1,1024]{3,2,1,0:T(1,128)S(1)} %copy.267, f32[16,4,7,1024]{3,2,1,0:T(8,128)S(1)} %slice.337, f32[16,4,8,1023]{3,2,1,0:T(8,128)S(1)} %slice.340, ...), kind=kLoop, calls=%fused_computation.100 | loop fusion | flops 14147584 | bytes 13922368 | tf_op jit(solution)/shard_map/reduce_sum | solution.py:126
  239.7 0.6 broadcast_multiply_fusion
  (88 shorter events, 7.7 us)
Async XLA Ops:
  0.6 24.1 %copy-start.11 = (s32[4,2]{0,1:T(2,128)S(1)}, s32[4,2]{0,1:T(2,128)}, u32[]{:S(2)}) copy-start(s32[4,2]{0,1:T(2,128)} %param.12) | copy-start | bytes 100
  1.5 25.9 %collective-permute-start = (f32[4,1024]{1,0:T(4,128)S(1)}, f32[4,1024]{1,0:T(4,128)S(1)}, u32[]{:S(2)}, u32[]{:S(2)}) collective-permute-start(f32[4,1024]{1,0:T(4,128)S(1)} %get-tuple-element.44), channel_id=1, source_target_pairs={{0,1},{1,2},{2,3},{3,4},{4,5},{5,6},{6,7},{7,8},{8,9},{9,10},{10,1... | collective-permute-start | bytes 49160 | tf_op jit(solution)/shard_map/ppermute | solution.py:18
  6.0 23.3 %collective-permute-start.2 = (f32[4,1024]{1,0:T(4,128)S(1)}, f32[4,1024]{1,0:T(4,128)S(1)}, u32[]{:S(2)}, u32[]{:S(2)}) collective-permute-start(f32[4,1024]{1,0:T(4,128)S(1)} %get-tuple-element.45), channel_id=1, source_target_pairs={{1,0},{2,1},{3,2},{4,3},{5,4},{6,5},{7,6},{8,7},{9,8},{10,9},{11,1... | collective-permute-start | bytes 49160 | tf_op jit(solution)/shard_map/ppermute | solution.py:21
  10.9 18.7 %collective-permute-start.1 = (f32[16,4,1,1024]{3,0,2,1:T(8,128)S(1)}, f32[16,4,1,1024]{3,0,2,1:T(8,128)}, u32[]{:S(2)}, u32[]{:S(2)}) collective-permute-start(f32[16,4,1,1024]{3,0,2,1:T(8,128)S(1)} %copy.269), channel_id=1, source_target_pairs={{0,1},{1,2},{2,3},{3,4},{4,5},{5,6},{6,7},{7,8},{8,9},{9,10},{10,1... | collective-permute-start | bytes 786440 | tf_op jit(solution)/shard_map/ppermute | solution.py:18
  15.4 10.9 %copy-start.12 = (s32[32,2]{0,1:T(2,128)S(1)}, s32[32,2]{0,1:T(2,128)}, u32[]{:S(2)}) copy-start(s32[32,2]{0,1:T(2,128)} %param.13) | copy-start | bytes 772
  15.4 11.1 %copy-start.16 = (f32[16]{0:T(128)S(1)}, f32[16]{0:T(128)}, u32[]{:S(2)}) copy-start(f32[16]{0:T(128)} %param.15) | copy-start | bytes 196
  15.4 15.4 %collective-permute-start.3 = (f32[16,4,1,1024]{3,0,2,1:T(8,128)}, f32[16,4,1,1024]{3,0,2,1:T(8,128)}, u32[]{:S(2)}, u32[]{:S(2)}) collective-permute-start(f32[16,4,1,1024]{3,0,2,1:T(8,128)} %copy.270), channel_id=1, source_target_pairs={{1,0},{2,1},{3,2},{4,3},{5,4},{6,5},{7,6},{8,7},{9,8},{10,9},{11,1... | collective-permute-start | bytes 786440 | tf_op jit(solution)/shard_map/ppermute | solution.py:21
  20.2 9.1 %copy-start.10 = (f32[8,1024]{1,0:T(8,128)S(1)}, f32[8,1024]{1,0:T(8,128)}, u32[]{:S(2)}) copy-start(f32[8,1024]{1,0:T(8,128)} %param.9) | copy-start | bytes 98308
  21.1 34.6 %collective-permute-start.9 = (f32[16,4,1,1024]{3,0,2,1:T(8,128)}, f32[16,4,1,1024]{3,0,2,1:T(8,128)}, u32[]{:S(2)}, u32[]{:S(2)}) collective-permute-start(f32[16,4,1,1024]{3,0,2,1:T(8,128)} %copy.272), channel_id=1, source_target_pairs={{0,1},{1,2},{2,3},{3,4},{4,5},{5,6},{6,7},{7,8},{8,9},{9,10},{10,1... | collective-permute-start | bytes 786440 | tf_op jit(solution)/shard_map/ppermute | solution.py:18
  25.6 6.4 %copy-start.9 = (f32[16,4,8,1024]{3,2,1,0:T(8,128)S(1)}, f32[16,4,8,1024]{3,2,1,0:T(8,128)}, u32[]{:S(2)}) copy-start(f32[16,4,8,1024]{3,2,1,0:T(8,128)} %param.10) | copy-start | bytes 6291460
  26.5 4.3 %copy-start.14 = (f32[16]{0:T(128)}, f32[16]{0:T(128)S(1)}, u32[]{:S(2)}) copy-start(f32[16]{0:T(128)S(1)} %mul.153) | copy-start | bytes 196
  27.4 30.4 %collective-permute-start.10 = (f32[16,4,1,1024]{3,0,2,1:T(8,128)}, f32[16,4,1,1024]{3,0,2,1:T(8,128)}, u32[]{:S(2)}, u32[]{:S(2)}) collective-permute-start(f32[16,4,1,1024]{3,0,2,1:T(8,128)} %copy.273), channel_id=1, source_target_pairs={{1,0},{2,1},{3,2},{4,3},{5,4},{6,5},{7,6},{8,7},{9,8},{10,9},{11,1... | collective-permute-start | bytes 786440 | tf_op jit(solution)/shard_map/ppermute | solution.py:21
  34.6 6.9 %collective-permute-start.4 = (f32[16,4,1,1024]{3,0,2,1:T(8,128)S(1)}, f32[16,4,1,1024]{3,0,2,1:T(8,128)S(1)}, u32[]{:S(2)}, u32[]{:S(2)}) collective-permute-start(f32[16,4,1,1024]{3,0,2,1:T(8,128)S(1)} %copy.240), channel_id=1, source_target_pairs={{0,1},{1,2},{2,3},{3,4},{4,5},{5,6},{6,7},{7,8},{8,9},{9,10},{10,1... | collective-permute-start | bytes 786440 | tf_op jit(solution)/shard_map/ppermute | solution.py:18
  38.5 7.7 %collective-permute-start.5 = (f32[16,4,1,1024]{3,0,2,1:T(8,128)S(1)}, f32[16,4,1,1024]{3,0,2,1:T(8,128)S(1)}, u32[]{:S(2)}, u32[]{:S(2)}) collective-permute-start(f32[16,4,1,1024]{3,0,2,1:T(8,128)S(1)} %copy.242), channel_id=1, source_target_pairs={{1,0},{2,1},{3,2},{4,3},{5,4},{6,5},{7,6},{8,7},{9,8},{10,9},{11,1... | collective-permute-start | bytes 786440 | tf_op jit(solution)/shard_map/ppermute | solution.py:21
  48.4 1.4 copy-start.4
  49.7 5.7 %copy-start.13 = (f32[4,32]{1,0:T(4,128)S(1)}, f32[4,32]{1,0:T(4,128)}, u32[]{:S(2)}) copy-start(f32[4,32]{1,0:T(4,128)} %param.14) | copy-start | bytes 1540
  49.8 5.8 %copy-start.17 = (f32[32]{0:T(128)S(1)}, f32[32]{0:T(128)}, u32[]{:S(2)}) copy-start(f32[32]{0:T(128)} %param.17) | copy-start | bytes 388
  49.8 5.8 %copy-start.18 = (f32[16]{0:T(128)S(1)}, f32[16]{0:T(128)}, u32[]{:S(2)}) copy-start(f32[16]{0:T(128)} %param.16) | copy-start | bytes 196
  50.4 9.3 %collective-permute-start.6 = (f32[16,4,1,1024]{3,0,2,1:T(8,128)S(1)}, f32[16,4,1,1024]{3,0,2,1:T(8,128)S(1)}, u32[]{:S(2)}, u32[]{:S(2)}) collective-permute-start(f32[16,4,1,1024]{3,0,2,1:T(8,128)S(1)} %copy.244), channel_id=1, source_target_pairs={{0,1},{1,2},{2,3},{3,4},{4,5},{5,6},{6,7},{7,8},{8,9},{9,10},{10,1... | collective-permute-start | bytes 786440 | tf_op jit(solution)/shard_map/ppermute | solution.py:18
  52.5 11.2 %collective-permute-start.7 = (f32[16,4,1,1024]{3,0,2,1:T(8,128)S(1)}, f32[16,4,1,1024]{3,0,2,1:T(8,128)S(1)}, u32[]{:S(2)}, u32[]{:S(2)}) collective-permute-start(f32[16,4,1,1024]{3,0,2,1:T(8,128)S(1)} %copy.246), channel_id=1, source_target_pairs={{1,0},{2,1},{3,2},{4,3},{5,4},{6,5},{7,6},{8,7},{9,8},{10,9},{11,1... | collective-permute-start | bytes 786440 | tf_op jit(solution)/shard_map/ppermute | solution.py:21
  55.6 8.4 %copy-start.5 = (f32[16,4,8,1024]{3,2,1,0:T(8,128)S(1)}, f32[16,4,8,1024]{3,2,1,0:T(8,128)}, u32[]{:S(2)}) copy-start(f32[16,4,8,1024]{3,2,1,0:T(8,128)} %copy-done.4) | copy-start | bytes 6291460
  65.9 161.3 %copy-start = (f32[16,4,8,1024]{3,2,1,0:T(8,128)}, f32[16,4,8,1024]{3,2,1,0:T(8,128)S(1)}, u32[]{:S(2)}) copy-start(f32[16,4,8,1024]{3,2,1,0:T(8,128)S(1)} %fusion.22) | copy-start | bytes 6291460
  194.0 12.4 %copy-start.3 = (f32[16,4,8,1024]{3,2,1,0:T(8,128)S(1)}, f32[16,4,8,1024]{3,2,1,0:T(8,128)}, u32[]{:S(2)}) copy-start(f32[16,4,8,1024]{3,2,1,0:T(8,128)} %copy.271) | copy-start | bytes 6291460
  194.7 9.7 %collective-permute-start.11 = (f32[16,4,1,1024]{3,0,2,1:T(8,128)S(1)}, f32[16,4,1,1024]{3,0,2,1:T(8,128)S(1)}, u32[]{:S(2)}, u32[]{:S(2)}) collective-permute-start(f32[16,4,1,1024]{3,0,2,1:T(8,128)S(1)} %copy.258), channel_id=1, source_target_pairs={{0,1},{1,2},{2,3},{3,4},{4,5},{5,6},{6,7},{7,8},{8,9},{9,10},{10,1... | collective-permute-start | bytes 786440 | tf_op jit(solution)/shard_map/ppermute | solution.py:18
  198.5 7.7 %collective-permute-start.12 = (f32[16,4,1,1024]{3,0,2,1:T(8,128)S(1)}, f32[16,4,1,1024]{3,0,2,1:T(8,128)S(1)}, u32[]{:S(2)}, u32[]{:S(2)}) collective-permute-start(f32[16,4,1,1024]{3,0,2,1:T(8,128)S(1)} %copy.260), channel_id=1, source_target_pairs={{1,0},{2,1},{3,2},{4,3},{5,4},{6,5},{7,6},{8,7},{9,8},{10,9},{11,1... | collective-permute-start | bytes 786440 | tf_op jit(solution)/shard_map/ppermute | solution.py:21
  209.1 9.0 %collective-permute-start.13 = (f32[16,4,1,1024]{3,0,2,1:T(8,128)S(1)}, f32[16,4,1,1024]{3,0,2,1:T(8,128)S(1)}, u32[]{:S(2)}, u32[]{:S(2)}) collective-permute-start(f32[16,4,1,1024]{3,0,2,1:T(8,128)S(1)} %copy.262), channel_id=1, source_target_pairs={{0,1},{1,2},{2,3},{3,4},{4,5},{5,6},{6,7},{7,8},{8,9},{9,10},{10,1... | collective-permute-start | bytes 786440 | tf_op jit(solution)/shard_map/ppermute | solution.py:18
  212.2 7.7 %collective-permute-start.14 = (f32[16,4,1,1024]{3,0,2,1:T(8,128)S(1)}, f32[16,4,1,1024]{3,0,2,1:T(8,128)S(1)}, u32[]{:S(2)}, u32[]{:S(2)}) collective-permute-start(f32[16,4,1,1024]{3,0,2,1:T(8,128)S(1)} %copy.264), channel_id=1, source_target_pairs={{1,0},{2,1},{3,2},{4,3},{5,4},{6,5},{7,6},{8,7},{9,8},{10,9},{11,1... | collective-permute-start | bytes 786440 | tf_op jit(solution)/shard_map/ppermute | solution.py:21
  215.2 14.7 %collective-permute-start.8 = (f32[16,4,1,1024]{3,0,2,1:T(8,128)}, f32[16,4,1,1024]{3,0,2,1:T(8,128)}, u32[]{:S(2)}, u32[]{:S(2)}) collective-permute-start(f32[16,4,1,1024]{3,0,2,1:T(8,128)} %copy.248), channel_id=1, source_target_pairs={{1,0},{2,1},{3,2},{4,3},{5,4},{6,5},{7,6},{8,7},{9,8},{10,9},{11,1... | collective-permute-start | bytes 786440 | tf_op jit(solution)/shard_map/ppermute | solution.py:29
  222.2 5.0 %copy-start.1 = (f32[16,4,8,1024]{3,2,1,0:T(8,128)}, f32[16,4,8,1024]{3,2,1,0:T(8,128)S(1)}, u32[]{:S(2)}) copy-start(f32[16,4,8,1024]{3,2,1,0:T(8,128)S(1)} %fusion.46) | copy-start | bytes 6291460
  223.5 10.4 %collective-permute-start.15 = (f32[16,4,1,1024]{3,0,2,1:T(8,128)}, f32[16,4,1,1024]{3,0,2,1:T(8,128)}, u32[]{:S(2)}, u32[]{:S(2)}) collective-permute-start(f32[16,4,1,1024]{3,0,2,1:T(8,128)} %copy.266), channel_id=1, source_target_pairs={{1,0},{2,1},{3,2},{4,3},{5,4},{6,5},{7,6},{8,7},{9,8},{10,9},{11,1... | collective-permute-start | bytes 786440 | tf_op jit(solution)/shard_map/ppermute | solution.py:29
  231.1 2.2 copy-start.2
  231.1 4.3 %copy-start.8 = (f32[16,4,8,1023]{3,2,1,0:T(8,128)S(1)}, f32[16,4,8,1023]{3,2,1,0:T(8,128)}, u32[]{:S(2)}) copy-start(f32[16,4,8,1023]{3,2,1,0:T(8,128)} %slice.339) | copy-start | bytes 6285316
  233.3 2.1 copy-start.6
  233.3 2.5 %copy-start.7 = (f32[16,4,7,1024]{3,2,1,0:T(8,128)S(1)}, f32[16,4,7,1024]{3,2,1,0:T(8,128)}, u32[]{:S(2)}) copy-start(f32[16,4,7,1024]{3,2,1,0:T(8,128)} %slice.330) | copy-start | bytes 5505028
  233.3 2.5 %copy-start.15 = (f32[16]{0:T(128)S(1)}, f32[16]{0:T(128)}, u32[]{:S(2)}) copy-start(f32[16]{0:T(128)} %copy-done.14) | copy-start | bytes 196
where the time goes:
time: 242 us; the launch traced here: 240 us
  local copies, waits for them, and re-layouts  92.1 us (38%)
  blocking collectives  54.2 us (22%)
  starting transfers between devices  44.7 us (18%)
  other arithmetic  33.5 us (14%)
  waiting for transfers between devices  14.5 us (6%)
    psum x1, blocking collectives, local(): predicted = lax.psum(partial_read, 'section')  54.2 us
    ppermute x7, starting transfers between devices, extended(): lax.ppermute(lax.slice_in_dim(block, block.shape[dim] - width, None, axis...  23.9 us
    add x6, other arithmetic, smooth_once(): (1.0 - OMEGA) * middle + OMEGA * (source_win + beside) / diag_terms[:, None]  17.1 us
    ppermute x7, starting transfers between devices, extended(): lax.ppermute(lax.slice_in_dim(block, 0, width, axis=dim), axis, backward)  16.8 us
    unnamed x45, local copies, waits for them, and re-layouts  16.5 us
    slice x1, local copies, waits for them, and re-layouts, sweep_all(): source_win = source_wide[:, :, SWEEPS:SWEEPS + row_count]  13.7 us
    ppermute x7, waiting for transfers between devices, extended(): lax.ppermute(lax.slice_in_dim(block, 0, width, axis=dim), axis, backward)  10.9 us
    broadcast_in_dim x1, local copies, waits for them, and re-layouts, local(): jnp.zeros(forward_start.shape[:2] + (span_wide, col_count), jnp.float32)  9.8 us
  transfers between devices with their start and end apart: 16, of which 7 were waited for; matrix products, arithmetic and copies ran while one was open for 15% of the time, Pallas kernels for 0%

commit v1 on v0

v1 whole, which is shorter than its diff:
```python
import functools

import jax
import jax.numpy as jnp
from jax import lax
from jax.experimental import pallas as pl
from jax.experimental.pallas import tpu as pltpu
from jax.sharding import PartitionSpec as P

SWEEPS = 3
OMEGA = 0.8
CURRENT = 10.0
ABOVE = SWEEPS
BELOW = SWEEPS + 1
LANES = 128


def split3(value):
    high = value.astype(jnp.bfloat16)
    rest = value - high.astype(jnp.float32)
    mid = rest.astype(jnp.bfloat16)
    low = (rest - mid.astype(jnp.float32)).astype(jnp.bfloat16)
    return high, mid, low


def kernel(
    count,
    steps,
    sigma_ref,
    fwd_ref,
    adj_ref,
    src_ref,
    rec_ref,
    obs_ref,
    wave_ref,
    quad_ref,
    off_ref,
    grad_ref,
    pred_ref,
    field_ref,
    sig,
    f0,
    a0,
    t1,
    t2,
    b1,
    b2,
    f3,
    a3,
    rd,
    fsrc,
    asrc,
    face_v,
    face_l,
    face_r,
    coef_s,
    wcol_s,
    oh_e,
    oh_t,
    lhs,
    parts,
    sig_send,
    sig_recv,
    up_send,
    up_recv,
    dn_send,
    dn_recv,
    red_send,
    red_recv,
    load_sem,
    store_sem,
):
    rows, cols = sigma_ref.shape
    fields = fwd_ref.shape[0]
    chunks = fields // 8
    wide = rows + 2 * SWEEPS - 1
    me = lax.axis_index("section")
    has_up = me > 0
    has_dn = me < count - 1
    start = me * rows

    def peer(step):
        bit = (me // (1 << step)) % 2
        return me + (1 - 2 * bit) * (1 << step)

    for which, (ref, buf) in enumerate(((fwd_ref, f0), (adj_ref, a0))):
        for j in range(rows):
            pltpu.make_async_copy(
                ref.at[:, j, :], buf.at[ABOVE + j], load_sem.at[which, j]
            ).start()

    @pl.when(jnp.logical_not(has_up))
    def _():
        sig[0:rows, :] = jnp.zeros((rows, cols), jnp.float32)
        f0[0:ABOVE] = jnp.zeros((ABOVE, fields, cols), jnp.float32)
        a0[0:ABOVE] = jnp.zeros((ABOVE, fields, cols), jnp.float32)

    @pl.when(jnp.logical_not(has_dn))
    def _():
        sig[2 * rows : 3 * rows, :] = jnp.zeros((rows, cols), jnp.float32)
        f0[ABOVE + rows :] = jnp.zeros((BELOW, fields, cols), jnp.float32)
        a0[ABOVE + rows :] = jnp.zeros((BELOW, fields, cols), jnp.float32)

    barrier = pltpu.get_barrier_semaphore()

    @pl.when(has_up)
    def _():
        pl.semaphore_signal(barrier, inc=1, device_id={"section": me - 1})

    @pl.when(has_dn)
    def _():
        pl.semaphore_signal(barrier, inc=1, device_id={"section": me + 1})

    for step in range(steps):
        pl.semaphore_signal(barrier, inc=1, device_id={"section": peer(step)})

    beside = 2 - (count - me) // count - (me + 1) // count
    pl.semaphore_wait(barrier, steps + beside)

    def sig_copy(side):
        place = (2 * rows, 0)[side]
        return pltpu.make_async_remote_copy(
            src_ref=sigma_ref,
            dst_ref=sig.at[pl.ds(place, rows)],
            send_sem=sig_send.at[side],
            recv_sem=sig_recv.at[side],
            device_id={"section": (me - 1, me + 1)[side]},
        )

    def up_copy(which, depth):
        ref, buf = ((fwd_ref, f0), (adj_ref, a0))[which]
        return pltpu.make_async_remote_copy(
            src_ref=ref.at[:, depth, :],
            dst_ref=buf.at[ABOVE + rows + depth],
            send_sem=up_send.at[which, depth],
            recv_sem=up_recv.at[which, depth],
            device_id={"section": me - 1},
        )

    def dn_copy(which, depth):
        ref, buf = ((fwd_ref, f0), (adj_ref, a0))[which]
        return pltpu.make_async_remote_copy(
            src_ref=ref.at[:, rows - 1 - depth, :],
            dst_ref=buf.at[ABOVE - 1 - depth],
            send_sem=dn_send.at[which, depth],
            recv_sem=dn_recv.at[which, depth],
            device_id={"section": me + 1},
        )

    order = [(0, d) for d in range(SWEEPS)] + [(1, d) for d in range(SWEEPS)]
    order += [(0, SWEEPS), (1, SWEEPS)]

    @pl.when(has_up)
    def _():
        sig_copy(0).start()
        for which, depth in order:
            up_copy(which, depth).start()

    @pl.when(has_dn)
    def _():
        sig_copy(1).start()
        for which, depth in order:
            if depth < SWEEPS:
                dn_copy(which, depth).start()

    lane = lax.broadcasted_iota(jnp.int32, (1, LANES), 1)
    eye = lax.broadcasted_iota(jnp.int32, (32, 32), 0) == lax.broadcasted_iota(
        jnp.int32, (32, 32), 1
    )
    rec = rec_ref[...].astype(jnp.float32)
    rec_m = jnp.sum(jnp.where(eye, rec[:, 0:1], 0.0), axis=0, keepdims=True)
    rec_n = jnp.sum(jnp.where(eye, rec[:, 1:2], 0.0), axis=0, keepdims=True)
    none = jnp.full((1, LANES - 64), -1.0, jnp.float32)
    cell_f = jnp.concatenate([rec_m, rec_n, none], axis=1)
    cell = cell_f.astype(jnp.int32)
    cell_row = jnp.where(cell < 0, -1000, cell // cols - start)
    cell_col = jnp.where(cell < 0, -1, cell % cols)
    eye_e = lax.broadcasted_iota(jnp.int32, (LANES, LANES), 0) == lax.broadcasted_iota(
        jnp.int32, (LANES, LANES), 1
    )
    col_down = jnp.sum(
        jnp.where(eye_e, cell_col.astype(jnp.float32), 0.0), axis=1, keepdims=True
    ).astype(jnp.int32)
    oh_e[...] = jnp.where(
        lax.broadcasted_iota(jnp.int32, (LANES, cols), 1) == col_down, 1.0, 0.0
    ).astype(jnp.bfloat16)
    oh_t[...] = jnp.where(
        lax.broadcasted_iota(jnp.int32, (cols, LANES), 0) == cell_col, 1.0, 0.0
    ).astype(jnp.bfloat16)

    kk = wave_ref.shape[1]
    srcs = fields // kk
    pick = lax.broadcasted_iota(jnp.int32, (fields, kk), 0) // srcs == lax.broadcasted_iota(
        jnp.int32, (fields, kk), 1
    )
    wave_col = jnp.sum(jnp.where(pick, wave_ref[...], 0.0), axis=1, keepdims=True)
    quad_col = jnp.sum(jnp.where(pick, quad_ref[...], 0.0), axis=1, keepdims=True)
    off = jnp.concatenate([off_ref[...]] * 4, axis=1)
    sign = jnp.where(lane < 32, 1.0, jnp.where(lane < 64, -1.0, 0.0))
    coef_s[...] = quad_col * jnp.cos(wave_col * off) * sign
    wcol_s[...] = jnp.broadcast_to(wave_col * wave_col, (fields, LANES))

    sig[rows : 2 * rows, :] = sigma_ref[...]

    @pl.when(has_dn)
    def _():
        sig_copy(0).wait_recv()

    @pl.when(has_up)
    def _():
        sig_copy(1).wait_recv()

    base = rows - (SWEEPS - 1)
    lane_c = lax.broadcasted_iota(jnp.int32, (8, cols), 1)
    src_a = jnp.concatenate([src_ref[:, 0:1]] * 2, axis=0)
    src_b = jnp.concatenate([src_ref[:, 1:2]] * 2, axis=0)
    for i in range(wide):
        r = i - (SWEEPS - 1)
        centre = jnp.broadcast_to(sig[base + i : base + i + 1, :], (8, cols))
        above = jnp.broadcast_to(sig[base + i - 1 : base + i, :], (8, cols))
        below = jnp.broadcast_to(sig[base + i + 1 : base + i + 2, :], (8, cols))
        v_up = 0.5 * (centre + above)
        v_dn = 0.5 * (centre + below)
        left = jnp.where(lane_c == 0, 0.0, pltpu.roll(centre, 1, 1))
        right = jnp.where(lane_c == cols - 1, 0.0, pltpu.roll(centre, cols - 1, 1))
        h_l = 0.5 * (centre + left)
        h_r = 0.5 * (centre + right)
        face_v[i] = v_up
        if i == wide - 1:
            face_v[i + 1] = v_dn
        face_l[i] = jnp.where(lane_c == 0, 0.0, h_l)
        face_r[i] = jnp.where(lane_c == cols - 1, 0.0, h_r)
        around = v_up + v_dn + h_l + h_r
        flat = (start + r) * cols + lane_c
        fsrc[i] = jnp.where(flat == src_a, CURRENT, 0.0) + jnp.where(flat == src_b, -CURRENT, 0.0)
        inside = jnp.logical_and(start + r >= 0, start + r < count * rows)
        scale = jnp.where(inside, OMEGA, 0.0)
        safe = jnp.where(inside, 0.0, 1.0)

        def fill(c, _, i=i, around=around, centre=centre, scale=scale, safe=safe):
            ks = pl.ds(pl.multiple_of(c * 8, 8), 8)
            w2 = wcol_s[ks, 0:1]
            rd[i, ks, :] = scale / (around + w2 * centre + safe)
            return 0

        lax.fori_loop(0, chunks, fill, 0)

    def update(src, dst, shift, source, r):
        i = r + (SWEEPS - 1)

        def body(c, _):
            ks = pl.ds(pl.multiple_of(c * 8, 8), 8)
            u = src[r + ABOVE, ks, :]
            f = fsrc[i] if source is None else source[i, ks, :]
            acc = f + face_v[i] * src[r + ABOVE - 1, ks, :]
            acc = acc + face_v[i + 1] * src[r + ABOVE + 1, ks, :]
            acc = acc + face_l[i] * pltpu.roll(u, 1, 1)
            acc = acc + face_r[i] * pltpu.roll(u, cols - 1, 1)
            dst[r + shift, ks, :] = (1.0 - OMEGA) * u + acc * rd[i, ks, :]
            return 0

        lax.fori_loop(0, chunks, body, 0)

    def span(level, lo, number, stride):
        src, dst, shift, source = level

        def body(j, _):
            update(src, dst, shift, source, lo + j * stride)
            return 0

        lax.fori_loop(0, number, body, 0)

    def sweeps(which, first, last, source, upto):
        one, two = ((t1, t2), (b1, b2))[which]
        levels = (
            (first, one, ABOVE, source),
            (one, two, ABOVE, source),
            (two, last, 0, source),
        )
        ref, buf = ((fwd_ref, f0), (adj_ref, a0))[which]
        for depth in upto:
            if depth == 0:
                for j in range(rows):
                    pltpu.make_async_copy(
                        ref.at[:, j, :], buf.at[ABOVE + j], load_sem.at[which, j]
                    ).wait()
                for t in range(SWEEPS):
                    span(levels[t], 1 + t, rows - 2 - 2 * t, 1)
                continue

            @pl.when(has_dn)
            def _(depth=depth):
                up_copy(which, depth - 1).wait_recv()

            if depth <= SWEEPS:

                @pl.when(has_up)
                def _(depth=depth):
                    dn_copy(which, depth - 1).wait_recv()

            for t in range(SWEEPS):
                low = 1 + t - depth
                high = rows - 2 - t + depth
                if depth <= SWEEPS:
                    span(levels[t], low, 2, high - low)
                else:
                    span(levels[t], high, 1, 1)

    sweeps(0, f0, f3, None, range(SWEEPS + 1))

    for j in range(rows):
        pltpu.make_async_copy(f3.at[j], field_ref.at[:, j, :], store_sem.at[j]).start()

    def read(j, total):
        value = jnp.zeros((fields, LANES), jnp.float32)
        for piece in split3(f3[j]):
            value = value + jnp.dot(piece, oh_t[...], preferred_element_type=jnp.float32)
        return total + jnp.where(cell_row == j, value, 0.0)

    got = lax.fori_loop(0, rows, read, jnp.zeros((fields, LANES), jnp.float32))
    got = got * coef_s[...]
    total = got[0:8]
    for c in range(1, chunks):
        total = total + got[8 * c : 8 * c + 8]
    total = total + pltpu.roll(total, 4, 0)
    for step in range(steps):
        parts[2 * step] = total
        copy = pltpu.make_async_remote_copy(
            src_ref=parts.at[2 * step],
            dst_ref=parts.at[2 * step + 1],
            send_sem=red_send.at[step],
            recv_sem=red_recv.at[step],
            device_id={"section": peer(step)},
        )
        copy.start()
        copy.wait()
        total = parts[2 * step] + parts[2 * step + 1]
    both = jnp.where(
        lane < 32, total + pltpu.roll(total, LANES - 32, 1), total + pltpu.roll(total, 32, 1)
    )
    pred_ref[...] = both[0:4, 0:32]
    obs = jnp.concatenate([obs_ref[...]] * 4, axis=1)
    obs = jnp.concatenate([obs] * 2, axis=0)
    miss = both - obs
    amp = coef_s[...] * jnp.concatenate([miss] * chunks, axis=0)
    pieces = split3(amp)
    for i in range(wide):
        keep = cell_row == i - (SWEEPS - 1)
        for p in range(3):
            lhs[p, i * fields : (i + 1) * fields, :] = jnp.where(
                keep, pieces[p], jnp.zeros_like(pieces[p])
            )

    def inject(i, _):
        at = pl.ds(pl.multiple_of(i * fields, fields), fields)
        value = jnp.zeros((fields, cols), jnp.float32)
        for p in range(3):
            value = value + jnp.dot(lhs[p, at, :], oh_e[...], preferred_element_type=jnp.float32)
        asrc[i] = value
        return 0

    lax.fori_loop(0, wide, inject, 0)

    def gradient(j):
        def body(c, acc):
            ks = pl.ds(pl.multiple_of(c * 8, 8), 8)
            f = f3[j, ks, :]
            a = a3[j, ks, :]
            fn = jnp.where(lane_c == cols - 1, 0.0, pltpu.roll(f, cols - 1, 1))
            an = jnp.where(lane_c == cols - 1, 0.0, pltpu.roll(a, cols - 1, 1))
            term = (f3[j + 1, ks, :] - f) * (a3[j + 1, ks, :] - a)
            term = term + (fn - f) * (an - a) + wcol_s[ks, 0:1] * (f * a)
            return acc + term

        acc = lax.fori_loop(0, chunks, body, jnp.zeros((8, cols), jnp.float32))
        return jnp.sum(acc, axis=0, keepdims=True) * (1.0 / srcs)

    sweeps(1, a0, a3, asrc, range(SWEEPS + 1))
    for j in range(rows - 1):
        if j == rows - 2:
            sweeps(0, f0, f3, None, (SWEEPS + 1,))
        grad_ref[j : j + 1, :] = gradient(j)
    sweeps(1, a0, a3, asrc, (SWEEPS + 1,))
    grad_ref[rows - 1 : rows, :] = gradient(rows - 1)

    @pl.when(has_up)
    def _():
        sig_copy(0).wait_send()
        for which, depth in order:
            up_copy(which, depth).wait_send()

    @pl.when(has_dn)
    def _():
        sig_copy(1).wait_send()
        for which, depth in order:
            if depth < SWEEPS:
                dn_copy(which, depth).wait_send()

    for j in range(rows):
        pltpu.make_async_copy(f3.at[j], field_ref.at[:, j, :], store_sem.at[j]).wait()


def solution(mesh):
    count = mesh.shape["section"]
    steps = count.bit_length() - 1

    def local(sigma, fwd, adj, src, rec, obs, wave, quad, off):
        kk, srcs, rows, cols = fwd.shape
        fields = kk * srcs
        deep = rows + ABOVE + BELOW
        wide = rows + 2 * SWEEPS - 1
        f32 = jnp.float32
        vmem = pl.BlockSpec(memory_space=pltpu.VMEM)
        anywhere = pl.BlockSpec(memory_space=pl.ANY)
        dma = pltpu.SemaphoreType.DMA
        grad, pred, field = pl.pallas_call(
            functools.partial(kernel, count, steps),
            out_shape=(
                jax.ShapeDtypeStruct((rows, cols), f32),
                jax.ShapeDtypeStruct(obs.shape, f32),
                jax.ShapeDtypeStruct((fields, rows, cols), f32),
            ),
            in_specs=[vmem, anywhere, anywhere] + [vmem] * 6,
            out_specs=(vmem, vmem, anywhere),
            scratch_shapes=[
                pltpu.VMEM((3 * rows, cols), f32),
                pltpu.VMEM((deep, fields, cols), f32),
                pltpu.VMEM((deep, fields, cols), f32),
                pltpu.VMEM((deep, fields, cols), f32),
                pltpu.VMEM((deep, fields, cols), f32),
                pltpu.VMEM((deep, fields, cols), f32),
                pltpu.VMEM((deep, fields, cols), f32),
                pltpu.VMEM((rows + 1, fields, cols), f32),
                pltpu.VMEM((rows + 1, fields, cols), f32),
                pltpu.VMEM((wide, fields, cols), f32),
                pltpu.VMEM((wide, 8, cols), f32),
                pltpu.VMEM((wide, fields, cols), f32),
                pltpu.VMEM((wide + 1, 8, cols), f32),
                pltpu.VMEM((wide, 8, cols), f32),
                pltpu.VMEM((wide, 8, cols), f32),
                pltpu.VMEM((fields, LANES), f32),
                pltpu.VMEM((fields, LANES), f32),
                pltpu.VMEM((LANES, cols), jnp.bfloat16),
                pltpu.VMEM((cols, LANES), jnp.bfloat16),
                pltpu.VMEM((3, wide * fields, LANES), jnp.bfloat16),
                pltpu.VMEM((2 * steps, 8, LANES), f32),
                dma((2,)),
                dma((2,)),
                dma((2, BELOW)),
                dma((2, BELOW)),
                dma((2, ABOVE)),
                dma((2, ABOVE)),
                dma((steps,)),
                dma((steps,)),
                dma((2, rows)),
                dma((rows,)),
            ],
            compiler_params=pltpu.CompilerParams(
                collective_id=0, has_side_effects=True, vmem_limit_bytes=48 << 20
            ),
        )(
            sigma,
            fwd.reshape(fields, rows, cols),
            adj.reshape(fields, rows, cols),
            src,
            rec,
            obs,
            wave.reshape(1, kk),
            quad.reshape(1, kk),
            off.reshape(1, off.shape[0]),
        )
        return grad, pred, field.reshape(fwd.shape)

    placed = (
        P(("line", "section"), None),
        P("line", None, "section", None),
        P("line", None, "section", None),
        P("line", None),
        P("line", None),
        P("line", None),
        P(),
        P(),
        P(),
    )
    return jax.shard_map(
        local,
        mesh=mesh,
        in_specs=placed,
        out_specs=(P(("line", "section"), None), P("line", None), P("line", None, "section", None)),
        check_vma=False,
    )
```

time: 242 us -> 114 us (0.47)
  the two profiles are of different devices: /device:TPU:1 before, /device:TPU:0 now
where the time goes in v1:
time: 114 us; the launch traced here: 113 us
  Pallas kernels  104 us (91%)
  local copies, waits for them, and re-layouts  9.03 us (8%)
    pallas_call x1, Pallas kernels, local(): pl.pallas_call(functools.partial(kernel, count, steps), out_shape=(jax.Sh...  104 us
    unnamed x17, local copies, waits for them, and re-layouts  9.03 us

profile of v1, /device:TPU:0, one launch (start us, length us, event | category | flops | bytes accessed | tf_op | source)
XLA Modules:
  0.0 113.3 jit_solution(4439455857835751266)
XLA Ops:
  0.6 0.8 copy.12.src_ref
  1.4 0.8 copy.13.rec_ref
  2.2 0.0 copy-start
  2.2 1.6 %copy-done = f32[16,4,8,1024]{3,2,1,0:T(8,128)S(1)} copy-done((f32[16,4,8,1024]{3,2,1,0:T(8,128)S(1)}, f32[16,4,8,1024]{3,2,1,0:T(8,128)}, u32[]{:S(2)}) %copy-start) | copy-done | bytes 2097176
  3.7 0.0 copy-start.1
  3.7 0.8 copy-done.1
  4.5 0.0 copy-start.2
  4.5 0.7 copy-done.2
  5.2 0.0 copy-start.3
  5.2 0.7 copy-done.3
  5.8 0.0 copy-start.4
  5.8 0.7 copy-done.4
  6.5 0.0 copy-start.5
  6.5 0.7 copy-done.5
  7.2 103.6 %shard_map.112 = (f32[8,1024]{1,0:T(8,128)S(1)}, f32[4,32]{1,0:T(4,128)S(1)}, f32[64,8,1024]{2,1,0:T(8,128)S(1)}) custom-call(f32[8,1024]{1,0:T(8,128)S(1)} %copy-done.1, f32[64,8,1024]{2,1,0:T(8,128)S(1)} %bitcast.6, f32[64,8,1024]{2,1,0:T(8,128)} %bitcast.11, s32[4,2]{1,0:T(4,128)S(1)} %copy.12.src_ref, s32[32,2]{1,0:T(8,128)S(1)} %copy.13.rec_ref, ...), custom_call_target="tpu_custom_call" | custom-call | tf_op jit(solution)/shard_map/pallas_call | solution.py:416
  110.8 0.6 copy.17
  111.4 0.6 copy.18
  112.0 1.3 %copy.19 = f32[16,4,8,1024]{3,2,1,0:T(8,128)} copy(f32[16,4,8,1024]{3,2,1,0:T(8,128)S(1)} %bitcast.7) | data formatting | bytes 4194304
Async XLA Ops:
  2.2 1.6 %copy-start = (f32[16,4,8,1024]{3,2,1,0:T(8,128)S(1)}, f32[16,4,8,1024]{3,2,1,0:T(8,128)}, u32[]{:S(2)}) copy-start(f32[16,4,8,1024]{3,2,1,0:T(8,128)} %param.10) | copy-start | bytes 6291460
  3.7 0.8 copy-start.1
  4.5 0.7 copy-start.2
  5.2 0.7 copy-start.3
  5.8 0.7 copy-start.4
  6.5 0.7 copy-start.5

commit v2 on v1

--- a/solution.py
+++ b/solution.py
@@ -38,6 +38,12 @@
     grad_ref,
     pred_ref,
     field_ref,
+    src_v,
+    rec_v,
+    obs_v,
+    wave_v,
+    quad_v,
+    off_v,
     sig,
     f0,
     a0,
@@ -69,6 +75,7 @@
     red_recv,
     load_sem,
     store_sem,
+    small_sem,
 ):
     rows, cols = sigma_ref.shape
     fields = fwd_ref.shape[0]
@@ -83,6 +90,18 @@
         bit = (me // (1 << step)) % 2
         return me + (1 - 2 * bit) * (1 << step)
 
+    small = (
+        (src_ref, src_v),
+        (rec_ref, rec_v),
+        (obs_ref, obs_v),
+        (wave_ref, wave_v),
+        (quad_ref, quad_v),
+        (off_ref, off_v),
+        (sigma_ref, sig.at[pl.ds(rows, rows)]),
+    )
+    for i, (ref, buf) in enumerate(small):
+        pltpu.make_async_copy(ref, buf, small_sem.at[i]).start()
+
     for which, (ref, buf) in enumerate(((fwd_ref, f0), (adj_ref, a0))):
         for j in range(rows):
             pltpu.make_async_copy(
@@ -163,13 +182,13 @@
             if depth < SWEEPS:
                 dn_copy(which, depth).start()
 
+    for i, (ref, buf) in enumerate(small):
+        pltpu.make_async_copy(ref, buf, small_sem.at[i]).wait()
+
     lane = lax.broadcasted_iota(jnp.int32, (1, LANES), 1)
-    eye = lax.broadcasted_iota(jnp.int32, (32, 32), 0) == lax.broadcasted_iota(
-        jnp.int32, (32, 32), 1
-    )
-    rec = rec_ref[...].astype(jnp.float32)
-    rec_m = jnp.sum(jnp.where(eye, rec[:, 0:1], 0.0), axis=0, keepdims=True)
-    rec_n = jnp.sum(jnp.where(eye, rec[:, 1:2], 0.0), axis=0, keepdims=True)
+    rec = rec_v[...].astype(jnp.float32)
+    rec_m = rec[0:1]
+    rec_n = rec[1:2]
     none = jnp.full((1, LANES - 64), -1.0, jnp.float32)
     cell_f = jnp.concatenate([rec_m, rec_n, none], axis=1)
     cell = cell_f.astype(jnp.int32)
@@ -188,19 +207,18 @@
         lax.broadcasted_iota(jnp.int32, (cols, LANES), 0) == cell_col, 1.0, 0.0
     ).astype(jnp.bfloat16)
 
-    kk = wave_ref.shape[1]
+    kk = wave_v.shape[1]
     srcs = fields // kk
     pick = lax.broadcasted_iota(jnp.int32, (fields, kk), 0) // srcs == lax.broadcasted_iota(
         jnp.int32, (fields, kk), 1
     )
-    wave_col = jnp.sum(jnp.where(pick, wave_ref[...], 0.0), axis=1, keepdims=True)
-    quad_col = jnp.sum(jnp.where(pick, quad_ref[...], 0.0), axis=1, keepdims=True)
-    off = jnp.concatenate([off_ref[...]] * 4, axis=1)
+    wave_col = jnp.sum(jnp.where(pick, wave_v[...], 0.0), axis=1, keepdims=True)
+    quad_col = jnp.sum(jnp.where(pick, quad_v[...], 0.0), axis=1, keepdims=True)
+    off = jnp.concatenate([off_v[...]] * 4, axis=1)
     sign = jnp.where(lane < 32, 1.0, jnp.where(lane < 64, -1.0, 0.0))
     coef_s[...] = quad_col * jnp.cos(wave_col * off) * sign
     wcol_s[...] = jnp.broadcast_to(wave_col * wave_col, (fields, LANES))
 
-    sig[rows : 2 * rows, :] = sigma_ref[...]
 
     @pl.when(has_dn)
     def _():
@@ -212,8 +230,12 @@
 
     base = rows - (SWEEPS - 1)
     lane_c = lax.broadcasted_iota(jnp.int32, (8, cols), 1)
-    src_a = jnp.concatenate([src_ref[:, 0:1]] * 2, axis=0)
-    src_b = jnp.concatenate([src_ref[:, 1:2]] * 2, axis=0)
+    own = lax.broadcasted_iota(jnp.int32, (8, srcs), 0) % srcs == lax.broadcasted_iota(
+        jnp.int32, (8, srcs), 1
+    )
+    src = src_v[...].astype(jnp.float32)
+    src_a = jnp.sum(jnp.where(own, src[0:1], 0.0), axis=1, keepdims=True).astype(jnp.int32)
+    src_b = jnp.sum(jnp.where(own, src[1:2], 0.0), axis=1, keepdims=True).astype(jnp.int32)
     for i in range(wide):
         r = i - (SWEEPS - 1)
         centre = jnp.broadcast_to(sig[base + i : base + i + 1, :], (8, cols))
@@ -243,7 +265,7 @@
             rd[i, ks, :] = scale / (around + w2 * centre + safe)
             return 0
 
-        lax.fori_loop(0, chunks, fill, 0)
+        lax.fori_loop(0, chunks, fill, 0, unroll=True)
 
     def update(src, dst, shift, source, r):
         i = r + (SWEEPS - 1)
@@ -259,7 +281,7 @@
             dst[r + shift, ks, :] = (1.0 - OMEGA) * u + acc * rd[i, ks, :]
             return 0
 
-        lax.fori_loop(0, chunks, body, 0)
+        lax.fori_loop(0, chunks, body, 0, unroll=True)
 
     def span(level, lo, number, stride):
         src, dst, shift, source = level
@@ -339,7 +361,7 @@
         lane < 32, total + pltpu.roll(total, LANES - 32, 1), total + pltpu.roll(total, 32, 1)
     )
     pred_ref[...] = both[0:4, 0:32]
-    obs = jnp.concatenate([obs_ref[...]] * 4, axis=1)
+    obs = jnp.concatenate([obs_v[...]] * 4, axis=1)
     obs = jnp.concatenate([obs] * 2, axis=0)
     miss = both - obs
     amp = coef_s[...] * jnp.concatenate([miss] * chunks, axis=0)
@@ -372,7 +394,7 @@
             term = term + (fn - f) * (an - a) + wcol_s[ks, 0:1] * (f * a)
             return acc + term
 
-        acc = lax.fori_loop(0, chunks, body, jnp.zeros((8, cols), jnp.float32))
+        acc = lax.fori_loop(0, chunks, body, jnp.zeros((8, cols), jnp.float32), unroll=True)
         return jnp.sum(acc, axis=0, keepdims=True) * (1.0 / srcs)
 
     sweeps(1, a0, a3, asrc, range(SWEEPS + 1))
@@ -420,9 +442,15 @@
                 jax.ShapeDtypeStruct(obs.shape, f32),
                 jax.ShapeDtypeStruct((fields, rows, cols), f32),
             ),
-            in_specs=[vmem, anywhere, anywhere] + [vmem] * 6,
+            in_specs=[anywhere] * 9,
             out_specs=(vmem, vmem, anywhere),
             scratch_shapes=[
+                pltpu.VMEM((2, src.shape[0]), jnp.int32),
+                pltpu.VMEM((2, rec.shape[0]), jnp.int32),
+                pltpu.VMEM(obs.shape, f32),
+                pltpu.VMEM((1, kk), f32),
+                pltpu.VMEM((1, kk), f32),
+                pltpu.VMEM((1, off.shape[0]), f32),
                 pltpu.VMEM((3 * rows, cols), f32),
                 pltpu.VMEM((deep, fields, cols), f32),
                 pltpu.VMEM((deep, fields, cols), f32),
@@ -454,6 +482,7 @@
                 dma((steps,)),
                 dma((2, rows)),
                 dma((rows,)),
+                dma((7,)),
             ],
             compiler_params=pltpu.CompilerParams(
                 collective_id=0, has_side_effects=True, vmem_limit_bytes=48 << 20
@@ -462,8 +491,8 @@
             sigma,
             fwd.reshape(fields, rows, cols),
             adj.reshape(fields, rows, cols),
-            src,
-            rec,
+            src.T,
+            rec.T,
             obs,
             wave.reshape(1, kk),
             quad.reshape(1, kk),

time: 114 us -> 77.2 us (0.68)
  Pallas kernels: 104 us -> 67.3 us
    pallas_call x1, Pallas kernels: 104 us -> 67.3 us  [local(): pl.pallas_call(functools.partial(kernel, count, steps), out_shape=(jax.Sh...]
    unnamed x17 -> x19, local copies, waits for them, and re-layouts: 9.03 us -> 8.86 us
where the time goes in v2:
time: 77.2 us; the launch traced here: 76.8 us
  Pallas kernels  67.3 us (87%)
  local copies, waits for them, and re-layouts  8.86 us (11%)
    pallas_call x1, Pallas kernels, local(): pl.pallas_call(functools.partial(kernel, count, steps), out_shape=(jax.Sh...  67.3 us
    unnamed x19, local copies, waits for them, and re-layouts  8.86 us

profile of v2, /device:TPU:0, one launch (start us, length us, event | category | flops | bytes accessed | tf_op | source)
XLA Modules:
  0.0 76.8 jit_solution(2200815455130874419)
XLA Ops:
  0.6 0.0 copy-start
  0.6 1.6 %copy-done = f32[16,4,8,1024]{3,2,1,0:T(8,128)S(1)} copy-done((f32[16,4,8,1024]{3,2,1,0:T(8,128)S(1)}, f32[16,4,8,1024]{3,2,1,0:T(8,128)}, u32[]{:S(2)}) %copy-start) | copy-done | bytes 2097176
  2.2 0.0 copy-start.1
  2.2 0.8 copy-done.1
  3.0 0.0 copy-start.2
  3.0 0.7 copy-done.2
  3.7 0.0 copy-start.3
  3.7 0.7 copy-done.3
  4.3 0.0 copy-start.4
  4.3 0.7 copy-done.4
  5.0 0.0 copy-start.5
  5.0 0.7 copy-done.5
  5.7 0.0 copy-start.6
  5.7 0.7 copy-done.6
  6.3 0.0 copy-start.7
  6.3 0.7 copy-done.7
  7.0 67.3 %shard_map.112 = (f32[8,1024]{1,0:T(8,128)S(1)}, f32[4,32]{1,0:T(4,128)S(1)}, f32[64,8,1024]{2,1,0:T(8,128)S(1)}) custom-call(f32[8,1024]{1,0:T(8,128)S(1)} %copy-done.1, f32[64,8,1024]{2,1,0:T(8,128)S(1)} %bitcast.8, f32[64,8,1024]{2,1,0:T(8,128)} %bitcast.15, s32[2,4]{1,0:T(2,128)S(1)} %bitcast.10, s32[2,32]{1,0:T(2,128)S(1)} %bitcast.11, ...), custom_call_target="tpu_custom_call" | custom-call | tf_op jit(solution)/shard_map/pallas_call | solution.py:438
  74.3 0.6 copy.15
  75.0 0.6 copy.16
  75.5 1.3 %copy.17 = f32[16,4,8,1024]{3,2,1,0:T(8,128)} copy(f32[16,4,8,1024]{3,2,1,0:T(8,128)S(1)} %bitcast.9) | data formatting | bytes 4194304
Async XLA Ops:
  0.6 1.6 %copy-start = (f32[16,4,8,1024]{3,2,1,0:T(8,128)S(1)}, f32[16,4,8,1024]{3,2,1,0:T(8,128)}, u32[]{:S(2)}) copy-start(f32[16,4,8,1024]{3,2,1,0:T(8,128)} %param.10) | copy-start | bytes 6291460
  2.2 0.8 copy-start.1
  3.0 0.7 copy-start.2
  3.7 0.7 copy-start.3
  4.3 0.7 copy-start.4
  5.0 0.7 copy-start.5
  5.7 0.7 copy-start.6
  6.3 0.7 copy-start.7

commit v3 on v2

--- a/solution.py
+++ b/solution.py
@@ -12,6 +12,8 @@
 CURRENT = 10.0
 ABOVE = SWEEPS
 BELOW = SWEEPS + 1
+LATER = (((1, 0),), ((1, 1),), ())
+LAST = ((1, 2), (0, 3), (1, 3))
 LANES = 128
 
 
@@ -172,15 +174,24 @@
     @pl.when(has_up)
     def _():
         sig_copy(0).start()
-        for which, depth in order:
-            up_copy(which, depth).start()
 
     @pl.when(has_dn)
     def _():
         sig_copy(1).start()
-        for which, depth in order:
-            if depth < SWEEPS:
-                dn_copy(which, depth).start()
+
+    def send(pairs):
+        @pl.when(has_up)
+        def _():
+            for which, depth in pairs:
+                up_copy(which, depth).start()
+
+        @pl.when(has_dn)
+        def _():
+            for which, depth in pairs:
+                if depth < SWEEPS:
+                    dn_copy(which, depth).start()
+
+    send(order[:SWEEPS])
 
     for i, (ref, buf) in enumerate(small):
         pltpu.make_async_copy(ref, buf, small_sem.at[i]).wait()
@@ -320,6 +331,9 @@
                 def _(depth=depth):
                     dn_copy(which, depth - 1).wait_recv()
 
+            if which == 0 and depth <= SWEEPS and LATER[depth - 1]:
+                send(LATER[depth - 1])
+
             for t in range(SWEEPS):
                 low = 1 + t - depth
                 high = rows - 2 - t + depth
@@ -357,6 +371,7 @@
         copy.start()
         copy.wait()
         total = parts[2 * step] + parts[2 * step + 1]
+    send(LAST)
     both = jnp.where(
         lane < 32, total + pltpu.roll(total, LANES - 32, 1), total + pltpu.roll(total, 32, 1)
     )
@@ -397,11 +412,13 @@
         acc = lax.fori_loop(0, chunks, body, jnp.zeros((8, cols), jnp.float32), unroll=True)
         return jnp.sum(acc, axis=0, keepdims=True) * (1.0 / srcs)
 
-    sweeps(1, a0, a3, asrc, range(SWEEPS + 1))
-    for j in range(rows - 1):
-        if j == rows - 2:
-            sweeps(0, f0, f3, None, (SWEEPS + 1,))
+    sweeps(1, a0, a3, asrc, range(SWEEPS))
+    for j in range(1, rows - 2):
         grad_ref[j : j + 1, :] = gradient(j)
+    sweeps(1, a0, a3, asrc, (SWEEPS,))
+    for j in (0, rows - 2):
+        grad_ref[j : j + 1, :] = gradient(j)
+    sweeps(0, f0, f3, None, (SWEEPS + 1,))
     sweeps(1, a0, a3, asrc, (SWEEPS + 1,))
     grad_ref[rows - 1 : rows, :] = gradient(rows - 1)
 

time: 77.2 us -> 67.1 us (0.87)
  Pallas kernels: 67.3 us -> 57.3 us
    pallas_call x1, Pallas kernels: 67.3 us -> 57.3 us  [local(): pl.pallas_call(functools.partial(kernel, count, steps), out_shape=(jax.Sh...]
where the time goes in v3:
time: 67.1 us; the launch traced here: 66.8 us
  Pallas kernels  57.3 us (85%)
  local copies, waits for them, and re-layouts  8.86 us (13%)
    pallas_call x1, Pallas kernels, local(): pl.pallas_call(functools.partial(kernel, count, steps), out_shape=(jax.Sh...  57.3 us
    unnamed x19, local copies, waits for them, and re-layouts  8.86 us

profile of v3, /device:TPU:0, one launch (start us, length us, event | category | flops | bytes accessed | tf_op | source)
XLA Modules:
  0.0 66.8 jit_solution(9968093999050272571)
XLA Ops:
  0.6 0.0 copy-start
  0.6 1.6 %copy-done = f32[16,4,8,1024]{3,2,1,0:T(8,128)S(1)} copy-done((f32[16,4,8,1024]{3,2,1,0:T(8,128)S(1)}, f32[16,4,8,1024]{3,2,1,0:T(8,128)}, u32[]{:S(2)}) %copy-start) | copy-done | bytes 2097176
  2.2 0.0 copy-start.1
  2.2 0.8 %copy-done.1 = f32[8,1024]{1,0:T(8,128)S(1)} copy-done((f32[8,1024]{1,0:T(8,128)S(1)}, f32[8,1024]{1,0:T(8,128)}, u32[]{:S(2)}) %copy-start.1) | copy-done | bytes 32792
  3.0 0.0 copy-start.2
  3.0 0.7 %copy-done.2 = f32[4,32]{1,0:T(4,128)S(1)} copy-done((f32[4,32]{1,0:T(4,128)S(1)}, f32[4,32]{1,0:T(4,128)}, u32[]{:S(2)}) %copy-start.2) | copy-done | bytes 536
  3.7 0.0 copy-start.3
  3.7 0.7 %copy-done.3 = s32[4,2]{0,1:T(2,128)S(1)} copy-done((s32[4,2]{0,1:T(2,128)S(1)}, s32[4,2]{0,1:T(2,128)}, u32[]{:S(2)}) %copy-start.3) | copy-done | bytes 56
  4.3 0.0 copy-start.4
  4.3 0.7 %copy-done.4 = s32[32,2]{0,1:T(2,128)S(1)} copy-done((s32[32,2]{0,1:T(2,128)S(1)}, s32[32,2]{0,1:T(2,128)}, u32[]{:S(2)}) %copy-start.4) | copy-done | bytes 280
  5.0 0.0 copy-start.5
  5.0 0.7 copy-done.5
  5.7 0.0 copy-start.6
  5.7 0.7 copy-done.6
  6.3 0.0 copy-start.7
  6.3 0.7 copy-done.7
  7.0 57.3 %shard_map.112 = (f32[8,1024]{1,0:T(8,128)S(1)}, f32[4,32]{1,0:T(4,128)S(1)}, f32[64,8,1024]{2,1,0:T(8,128)S(1)}) custom-call(f32[8,1024]{1,0:T(8,128)S(1)} %copy-done.1, f32[64,8,1024]{2,1,0:T(8,128)S(1)} %bitcast.8, f32[64,8,1024]{2,1,0:T(8,128)} %bitcast.15, s32[2,4]{1,0:T(2,128)S(1)} %bitcast.10, s32[2,32]{1,0:T(2,128)S(1)} %bitcast.11, ...), custom_call_target="tpu_custom_call" | custom-call | tf_op jit(solution)/shard_map/pallas_call | solution.py:455
  64.3 0.6 copy.15
  64.9 0.6 copy.16
  65.5 1.3 %copy.17 = f32[16,4,8,1024]{3,2,1,0:T(8,128)} copy(f32[16,4,8,1024]{3,2,1,0:T(8,128)S(1)} %bitcast.9) | data formatting | bytes 4194304
Async XLA Ops:
  0.6 1.6 %copy-start = (f32[16,4,8,1024]{3,2,1,0:T(8,128)S(1)}, f32[16,4,8,1024]{3,2,1,0:T(8,128)}, u32[]{:S(2)}) copy-start(f32[16,4,8,1024]{3,2,1,0:T(8,128)} %param.10) | copy-start | bytes 6291460
  2.2 0.8 %copy-start.1 = (f32[8,1024]{1,0:T(8,128)S(1)}, f32[8,1024]{1,0:T(8,128)}, u32[]{:S(2)}) copy-start(f32[8,1024]{1,0:T(8,128)} %sigma_ref.1) | copy-start | bytes 98308
  3.0 0.7 %copy-start.2 = (f32[4,32]{1,0:T(4,128)S(1)}, f32[4,32]{1,0:T(4,128)}, u32[]{:S(2)}) copy-start(f32[4,32]{1,0:T(4,128)} %obs_ref.1) | copy-start | bytes 1540
  3.7 0.7 %copy-start.3 = (s32[4,2]{0,1:T(2,128)S(1)}, s32[4,2]{0,1:T(2,128)}, u32[]{:S(2)}) copy-start(s32[4,2]{0,1:T(2,128)} %param.12) | copy-start | bytes 100
  4.3 0.7 %copy-start.4 = (s32[32,2]{0,1:T(2,128)S(1)}, s32[32,2]{0,1:T(2,128)}, u32[]{:S(2)}) copy-start(s32[32,2]{0,1:T(2,128)} %param.13) | copy-start | bytes 772
  5.0 0.7 copy-start.5
  5.7 0.7 copy-start.6
  6.3 0.7 copy-start.7
